TPU v7x, 32 devices: a whole 2x2x4 slice. The times are simulated.
32 devices in a mesh: group: 2 (over x), seq: 8 (over z, y), res: 2 (over core).
Axes of the slice: x: 2, y: 2, z: 4, core: 2. Of those that a mesh axis runs over, the one named last changes fastest.
Arguments:
- alignment: bfloat16 [1024, 128, 256], P(('group', 'seq'), 'res'), parts along dimension 0, may hold values from -8 to 8
- ln_gain: float32 [256], replicated, may hold values from 0.5 to 1.5
- ln_bias: float32 [256], replicated, may hold values from -0.6 to 0.6
- w_left: bfloat16 [256, 32], replicated, may hold values from -0.375 to 0.375
- bias_left: float32 [32], replicated, may hold values from -0.6 to 0.6
- w_right: bfloat16 [256, 32], replicated, may hold values from -0.375 to 0.375
- bias_right: float32 [32], replicated, may hold values from -0.6 to 0.6
- w_out: bfloat16 [1024, 128], replicated, may hold values from -1.5 to 1.5
- bias_out: float32 [128], replicated, may hold values from -0.5 to 0.5
Outputs:
- pair_update: bfloat16 [256, 128, 128], P(('group', 'seq'), 'res'), parts along dimension 0
There are 2 independent parts, one for each index of `group`. A program takes and returns all parts, laid end to end along the dimension named above; an argument that names none is the same for every part. Nothing has to cross between parts.
All inputs are finite; a program needn't handle non-finite values.
Results may differ from a plain program's by a relative error of at most 0.0034.
Values may be sent and summed in bfloat16 or wider, within the bound.
A program may use at most 64 MiB of HBM per device.

v0:
```python
import math

import jax
import jax.numpy as jnp
from jax import lax
from jax.sharding import PartitionSpec as P


def normalize(alignment, ln_gain, ln_bias):
    values = alignment.astype(jnp.float32)
    center = jnp.mean(values, axis=-1, keepdims=True)
    spread = jnp.mean(jnp.square(values - center), axis=-1, keepdims=True)
    return ((values - center) * lax.rsqrt(spread + 1e-05) * ln_gain + ln_bias).astype(jnp.bfloat16)


def project(normed, weight, offset):
    flattened = normed.reshape(-1, normed.shape[-1])
    return (jnp.dot(flattened, weight, preferred_element_type=jnp.float32) + offset).astype(
        jnp.bfloat16
    )


def pair_tile(left_rows, right_rows, weight_cube, rows_here):
    sequences = left_rows.shape[0]
    proj_width = weight_cube.shape[0]
    height = math.gcd(rows_here, 16)
    left_blocks = left_rows.reshape(sequences, rows_here // height, height, proj_width).transpose(
        1, 0, 2, 3
    )
    right_cube = right_rows.reshape(sequences, -1, proj_width)

    def one_block(left_block):
        outers = jnp.einsum(
            "sic,sje->icej", left_block, right_cube, preferred_element_type=jnp.float32
        ).astype(jnp.bfloat16)
        return jnp.einsum("icej,ceo->ijo", outers, weight_cube, preferred_element_type=jnp.float32)

    pieces = lax.map(one_block, left_blocks)
    return pieces.reshape(rows_here, right_cube.shape[1], weight_cube.shape[2])


def shards(alignment, ln_gain, ln_bias, w_left, bias_left, w_right, bias_right, w_out, bias_out):
    sequences = alignment.shape[0]
    residues = alignment.shape[1]
    proj_width = w_left.shape[1]
    out_width = w_out.shape[1]
    normed = normalize(alignment, ln_gain, ln_bias)
    left_rows = project(normed, w_left, bias_left).reshape(sequences, residues * proj_width)
    right_rows = project(normed, w_right, bias_right).reshape(sequences, residues * proj_width)
    weight_cube = w_out.reshape(proj_width, proj_width, out_width)
    columns = lax.all_gather(left_rows, "res", axis=1, tiled=True)
    width_all = columns.shape[1] // proj_width
    devices_seq = lax.axis_size("seq")
    kept_rows = width_all // devices_seq
    summed = lax.psum_scatter(
        pair_tile(columns, right_rows, weight_cube, lax.axis_size("seq") * kept_rows),
        "seq",
        scatter_dimension=0,
        tiled=True,
    )
    return (summed / (sequences * devices_seq) + bias_out).astype(jnp.bfloat16)


def solution(mesh):
    return jax.shard_map(
        shards,
        mesh=mesh,
        in_specs=(P(("group", "seq"), "res", None), P(), P(), P(), P(), P(), P(), P(), P()),
        out_specs=P(("group", "seq"), "res", None),
        check_vma=False,
    )
```

profile of v0, /device:TPU:0, one launch (start us, length us, event | category | flops | bytes accessed | tf_op | source)
XLA Modules:
  0.0 161.0 jit_solution(2791154676896824042)
XLA Ops:
  6.6 2.3 %convert_reduce_fusion = f32[64,64]{1,0:T(8,128)S(1)} fusion(bf16[64,64,256]{2,1,0:T(8,128)(2,1)} %param.11), kind=kLoop, calls=%fused_computation.10 | loop fusion | flops 2093056 | bytes 2113536 | tf_op jit(solution)/shard_map/reduce_sum | solution.py:11
  9.0 2.5 %fusion.16 = f32[64,64]{1,0:T(8,128)S(1)} fusion(bf16[64,64,256]{2,1,0:T(8,128)(2,1)} %param.11, f32[64,64]{1,0:T(8,128)S(1)} %broadcast_multiply_fusion), kind=kLoop, calls=%fused_computation.17 | loop fusion | flops 4190208 | bytes 2129920 | tf_op jit(solution)/shard_map/reduce_sum | solution.py:12
  11.6 1.5 fusion.19
  13.1 1.3 copy-done.2
  15.6 1.1 reshape.34
  16.7 2.4 %all_gather.3 = bf16[64,4096]{1,0:T(8,128)(2,1)} all-gather(bf16[64,2048]{1,0:T(8,128)(2,1)S(1)} %reshape.34), channel_id=1, replica_groups=mesh['group'=2,'seq'=8,'res'=2] {'res'}, dimensions={1}, use_global_device_ids=true | all-gather | bytes 786432 | tf_op jit(solution)/shard_map/all_gather | solution.py:51
  19.1 1.5 copy.12
  21.8 39.8 %while.10 = (s32[]{:T(128)}, f32[8,16,64,128]{3,2,1,0:T(8,128)}, bf16[8,64,16,32]{1,3,2,0:T(8,128)(2,1)S(1)}, bf16[64,64,32]{2,1,0:T(8,128)(2,1)S(1)}, bf16[32,32,128]{2,1,0:T(8,128)(2,1)}, /*index=5*/s32[]{:T(128)}) while((s32[]{:T(128)}, f32[8,16,64,128]{3,2,1,0:T(8,128)}, bf16[8,64,16,32]{1,3,2,0:T(8,128)(2,1)S(1)}, ...), condition=%wide.region_3.4_spmd, body=%wide.region_2.3_spmd.sunk | while | flops 402653184 | bytes 7144037 | solution.py:38
  23.1 1.3 fusion.35
  24.4 2.4 %fusion.36 = f32[8,16,64,128]{3,2,1,0:T(8,128)} fusion(f32[8,16,64,128]{3,2,1,0:T(8,128)} %get-tuple-element.91, s32[]{:T(128)} %get-tuple-element.90, bf16[16,32,64,32]{2,1,3,0:T(8,128)(2,1)S(1)} %fusion.35, bf16[32,32,128]{2,1,0:T(8,128)(2,1)S(1)} %copy-done.10), kind=kOutput, calls=%fused_computation.4.clone.1 | convolution fusion | flops 268435456 | bytes 2884096 | tf_op jit(solution)/shard_map/while/body/eval_jaxpr/icej,ceo->ijo/dot_general | solution.py:36
  27.1 1.0 copy.37
  28.1 1.3 fusion.35
  29.4 2.4 %fusion.36 = f32[8,16,64,128]{3,2,1,0:T(8,128)} fusion(f32[8,16,64,128]{3,2,1,0:T(8,128)} %get-tuple-element.91, s32[]{:T(128)} %get-tuple-element.90, bf16[16,32,64,32]{2,1,3,0:T(8,128)(2,1)S(1)} %fusion.35, bf16[32,32,128]{2,1,0:T(8,128)(2,1)S(1)} %copy-done.10), kind=kOutput, calls=%fused_computation.4.clone.1 | convolution fusion | flops 268435456 | bytes 2884096 | tf_op jit(solution)/shard_map/while/body/eval_jaxpr/icej,ceo->ijo/dot_general | solution.py:36
  32.1 1.0 copy.37
  33.0 1.3 fusion.35
  34.3 2.4 %fusion.36 = f32[8,16,64,128]{3,2,1,0:T(8,128)} fusion(f32[8,16,64,128]{3,2,1,0:T(8,128)} %get-tuple-element.91, s32[]{:T(128)} %get-tuple-element.90, bf16[16,32,64,32]{2,1,3,0:T(8,128)(2,1)S(1)} %fusion.35, bf16[32,32,128]{2,1,0:T(8,128)(2,1)S(1)} %copy-done.10), kind=kOutput, calls=%fused_computation.4.clone.1 | convolution fusion | flops 268435456 | bytes 2884096 | tf_op jit(solution)/shard_map/while/body/eval_jaxpr/icej,ceo->ijo/dot_general | solution.py:36
  37.0 1.0 copy.37
  38.0 1.3 fusion.35
  39.3 2.4 %fusion.36 = f32[8,16,64,128]{3,2,1,0:T(8,128)} fusion(f32[8,16,64,128]{3,2,1,0:T(8,128)} %get-tuple-element.91, s32[]{:T(128)} %get-tuple-element.90, bf16[16,32,64,32]{2,1,3,0:T(8,128)(2,1)S(1)} %fusion.35, bf16[32,32,128]{2,1,0:T(8,128)(2,1)S(1)} %copy-done.10), kind=kOutput, calls=%fused_computation.4.clone.1 | convolution fusion | flops 268435456 | bytes 2884096 | tf_op jit(solution)/shard_map/while/body/eval_jaxpr/icej,ceo->ijo/dot_general | solution.py:36
  42.0 1.0 copy.37
  43.0 1.3 fusion.35
  44.3 2.4 %fusion.36 = f32[8,16,64,128]{3,2,1,0:T(8,128)} fusion(f32[8,16,64,128]{3,2,1,0:T(8,128)} %get-tuple-element.91, s32[]{:T(128)} %get-tuple-element.90, bf16[16,32,64,32]{2,1,3,0:T(8,128)(2,1)S(1)} %fusion.35, bf16[32,32,128]{2,1,0:T(8,128)(2,1)S(1)} %copy-done.10), kind=kOutput, calls=%fused_computation.4.clone.1 | convolution fusion | flops 268435456 | bytes 2884096 | tf_op jit(solution)/shard_map/while/body/eval_jaxpr/icej,ceo->ijo/dot_general | solution.py:36
  47.0 1.0 copy.37
  47.9 1.3 fusion.35
  49.2 2.4 %fusion.36 = f32[8,16,64,128]{3,2,1,0:T(8,128)} fusion(f32[8,16,64,128]{3,2,1,0:T(8,128)} %get-tuple-element.91, s32[]{:T(128)} %get-tuple-element.90, bf16[16,32,64,32]{2,1,3,0:T(8,128)(2,1)S(1)} %fusion.35, bf16[32,32,128]{2,1,0:T(8,128)(2,1)S(1)} %copy-done.10), kind=kOutput, calls=%fused_computation.4.clone.1 | convolution fusion | flops 268435456 | bytes 2884096 | tf_op jit(solution)/shard_map/while/body/eval_jaxpr/icej,ceo->ijo/dot_general | solution.py:36
  52.0 1.0 copy.37
  52.9 1.3 fusion.35
  54.2 2.4 %fusion.36 = f32[8,16,64,128]{3,2,1,0:T(8,128)} fusion(f32[8,16,64,128]{3,2,1,0:T(8,128)} %get-tuple-element.91, s32[]{:T(128)} %get-tuple-element.90, bf16[16,32,64,32]{2,1,3,0:T(8,128)(2,1)S(1)} %fusion.35, bf16[32,32,128]{2,1,0:T(8,128)(2,1)S(1)} %copy-done.10), kind=kOutput, calls=%fused_computation.4.clone.1 | convolution fusion | flops 268435456 | bytes 2884096 | tf_op jit(solution)/shard_map/while/body/eval_jaxpr/icej,ceo->ijo/dot_general | solution.py:36
  57.9 1.3 fusion.35
  59.2 2.4 %fusion.36 = f32[8,16,64,128]{3,2,1,0:T(8,128)} fusion(f32[8,16,64,128]{3,2,1,0:T(8,128)} %get-tuple-element.91, s32[]{:T(128)} %get-tuple-element.90, bf16[16,32,64,32]{2,1,3,0:T(8,128)(2,1)S(1)} %fusion.35, bf16[32,32,128]{2,1,0:T(8,128)(2,1)S(1)} %copy-done.10), kind=kOutput, calls=%fused_computation.4.clone.1 | convolution fusion | flops 268435456 | bytes 2884096 | tf_op jit(solution)/shard_map/while/body/eval_jaxpr/icej,ceo->ijo/dot_general | solution.py:36
  61.6 90.7 %reduce-scatter.2.cloned.1.call-done = f32[16,64,128]{2,1,0:T(8,128)} async-done(((f32[128,64,128]{2,1,0:T(8,128)}), f32[16,64,128]{2,1,0:T(8,128)}) %reduce-scatter.2.cloned.1.call-update) | async-done | bytes 524304 | tf_op jit(solution)/shard_map/reduce_scatter | solution.py:55
  152.3 1.8 %add_convert_fusion = bf16[16,64,128]{2,1,0:T(8,128)(2,1)} fusion(f32[16,64,128]{2,1,0:T(8,128)} %reduce-scatter.2.cloned.1.call-done, f32[128]{0:T(128)S(1)} %copy-done.7), kind=kLoop, calls=%fused_computation.21 | loop fusion | flops 393216 | bytes 786944 | tf_op jit(solution)/shard_map/convert_element_type | solution.py:61
  (62 shorter events, 6.5 us)
Async XLA Ops:
  6.5 7.8 %copy-start = (bf16[256,32]{0,1:T(8,128)(2,1)S(1)}, bf16[256,32]{0,1:T(8,128)(2,1)}, u32[]{:S(2)}) copy-start(bf16[256,32]{0,1:T(8,128)(2,1)} %param.14) | copy-start | bytes 49156
  6.5 5.0 %copy-start.1 = (bf16[64,64,256]{2,1,0:T(8,128)(2,1)S(1)}, bf16[64,64,256]{2,1,0:T(8,128)(2,1)}, u32[]{:S(2)}) copy-start(bf16[64,64,256]{2,1,0:T(8,128)(2,1)} %param.11) | copy-start | bytes 6291460
  6.5 5.0 %copy-start.6 = (f32[256]{0:T(256)S(1)}, f32[256]{0:T(256)}, u32[]{:S(2)}) copy-start(f32[256]{0:T(256)} %param.12) | copy-start | bytes 3076
  6.5 5.0 %copy-start.5 = (f32[256]{0:T(256)S(1)}, f32[256]{0:T(256)}, u32[]{:S(2)}) copy-start(f32[256]{0:T(256)} %param.13) | copy-start | bytes 3076
  6.5 145.8 %reduce-scatter.2.cloned.1.call-start = ((), (), s32[]{:S(2)}) async-start(), calls=%async_computation.1 | async-start | bytes 4718592 | tf_op jit(solution)/shard_map/reduce_scatter | solution.py:55
  6.6 7.8 %copy-start.8 = (f32[32]{0:T(128)S(1)}, f32[32]{0:T(128)}, u32[]{:S(2)}) copy-start(f32[32]{0:T(128)} %param.15) | copy-start | bytes 388
  13.0 1.3 copy-start.2
  13.0 7.6 %copy-start.4 = (bf16[256,32]{0,1:T(8,128)(2,1)S(1)}, bf16[256,32]{0,1:T(8,128)(2,1)}, u32[]{:S(2)}) copy-start(bf16[256,32]{0,1:T(8,128)(2,1)} %param.16) | copy-start | bytes 49156
  13.1 7.6 %copy-start.9 = (f32[32]{0:T(128)S(1)}, f32[32]{0:T(128)}, u32[]{:S(2)}) copy-start(f32[32]{0:T(128)} %param.17) | copy-start | bytes 388
  15.1 5.6 %copy-start.3 = (bf16[64,64,256]{2,1,0:T(8,128)(2,1)S(1)}, bf16[64,64,256]{2,1,0:T(8,128)(2,1)}, u32[]{:S(2)}) copy-start(bf16[64,64,256]{2,1,0:T(8,128)(2,1)} %copy-done.2) | copy-start | bytes 6291460
  21.9 2.5 %copy-start.10 = (bf16[32,32,128]{2,1,0:T(8,128)(2,1)S(1)}, bf16[32,32,128]{2,1,0:T(8,128)(2,1)}, u32[]{:S(2)}) copy-start(bf16[32,32,128]{2,1,0:T(8,128)(2,1)} %get-tuple-element.100) | copy-start | bytes 786436 | tf_op jit(solution)/shard_map/while
  26.8 2.5 %copy-start.10 = (bf16[32,32,128]{2,1,0:T(8,128)(2,1)S(1)}, bf16[32,32,128]{2,1,0:T(8,128)(2,1)}, u32[]{:S(2)}) copy-start(bf16[32,32,128]{2,1,0:T(8,128)(2,1)} %get-tuple-element.100) | copy-start | bytes 786436 | tf_op jit(solution)/shard_map/while
  31.8 2.5 %copy-start.10 = (bf16[32,32,128]{2,1,0:T(8,128)(2,1)S(1)}, bf16[32,32,128]{2,1,0:T(8,128)(2,1)}, u32[]{:S(2)}) copy-start(bf16[32,32,128]{2,1,0:T(8,128)(2,1)} %get-tuple-element.100) | copy-start | bytes 786436 | tf_op jit(solution)/shard_map/while
  36.8 2.5 %copy-start.10 = (bf16[32,32,128]{2,1,0:T(8,128)(2,1)S(1)}, bf16[32,32,128]{2,1,0:T(8,128)(2,1)}, u32[]{:S(2)}) copy-start(bf16[32,32,128]{2,1,0:T(8,128)(2,1)} %get-tuple-element.100) | copy-start | bytes 786436 | tf_op jit(solution)/shard_map/while
  41.7 2.5 %copy-start.10 = (bf16[32,32,128]{2,1,0:T(8,128)(2,1)S(1)}, bf16[32,32,128]{2,1,0:T(8,128)(2,1)}, u32[]{:S(2)}) copy-start(bf16[32,32,128]{2,1,0:T(8,128)(2,1)} %get-tuple-element.100) | copy-start | bytes 786436 | tf_op jit(solution)/shard_map/while
  46.7 2.5 %copy-start.10 = (bf16[32,32,128]{2,1,0:T(8,128)(2,1)S(1)}, bf16[32,32,128]{2,1,0:T(8,128)(2,1)}, u32[]{:S(2)}) copy-start(bf16[32,32,128]{2,1,0:T(8,128)(2,1)} %get-tuple-element.100) | copy-start | bytes 786436 | tf_op jit(solution)/shard_map/while
  51.7 2.5 %copy-start.10 = (bf16[32,32,128]{2,1,0:T(8,128)(2,1)S(1)}, bf16[32,32,128]{2,1,0:T(8,128)(2,1)}, u32[]{:S(2)}) copy-start(bf16[32,32,128]{2,1,0:T(8,128)(2,1)} %get-tuple-element.100) | copy-start | bytes 786436 | tf_op jit(solution)/shard_map/while
  56.6 2.5 %copy-start.10 = (bf16[32,32,128]{2,1,0:T(8,128)(2,1)S(1)}, bf16[32,32,128]{2,1,0:T(8,128)(2,1)}, u32[]{:S(2)}) copy-start(bf16[32,32,128]{2,1,0:T(8,128)(2,1)} %get-tuple-element.100) | copy-start | bytes 786436 | tf_op jit(solution)/shard_map/while
  61.6 90.7 %copy-start.7 = (f32[128]{0:T(128)S(1)}, f32[128]{0:T(128)}, u32[]{:S(2)}) copy-start(f32[128]{0:T(128)} %param.19) | copy-start | bytes 1540
Sparse Core Ops, SparseCore 0:
  61.8 90.5 reduce-scatter.1
where the time goes:
time: 161 us
  waiting for transfers between devices  90.7 us (56%)
  matrix products  31.1 us (19%)
  local copies, waits for them, and re-layouts  14.7 us (9%)
  between operations  13.6 us (8%)
  other arithmetic  8.18 us (5%)
  blocking collectives  2.39 us (1%)
    reduce_scatter x1, waiting for transfers between devices, shards(): lax.psum_scatter(pair_tile(columns, right_rows, weight_cube, lax.axis_siz...  90.7 us
    dot_general x8, matrix products, one_block(): jnp.einsum('icej,ceo->ijo', outers, weight_cube, preferred_element_type=j...  19.5 us
    dot_general x8, matrix products, one_block(): jnp.einsum('sic,sje->icej', left_block, right_cube, preferred_element_typ...  10.2 us
    another operation x8, local copies, waits for them, and re-layouts  7.64 us
  transfers between devices with their start and end apart: 1, of which 1 were waited for; matrix products, arithmetic and copies ran while one was open for 0% of the time, Pallas kernels for 0%

commit v1 on v0

--- a/solution.py
+++ b/solution.py
@@ -1,9 +1,15 @@
+import functools
 import math
 
 import jax
 import jax.numpy as jnp
 from jax import lax
+from jax.experimental import pallas as pl
+from jax.experimental.pallas import tpu as pltpu
 from jax.sharding import PartitionSpec as P
+
+MESH = pl.DeviceIdType.MESH
+LANES = 128
 
 
 def normalize(alignment, ln_gain, ln_bias):
@@ -39,7 +45,7 @@
     return pieces.reshape(rows_here, right_cube.shape[1], weight_cube.shape[2])
 
 
-def shards(alignment, ln_gain, ln_bias, w_left, bias_left, w_right, bias_right, w_out, bias_out):
+def plain(alignment, ln_gain, ln_bias, w_left, bias_left, w_right, bias_right, w_out, bias_out):
     sequences = alignment.shape[0]
     residues = alignment.shape[1]
     proj_width = w_left.shape[1]
@@ -61,9 +67,333 @@
     return (summed / (sequences * devices_seq) + bias_out).astype(jnp.bfloat16)
 
 
+def fused_kernel(
+    dims,
+    a_hbm, gain_ref, beta_ref, wl_ref, bl_ref, wr_ref, br_ref, w_ref, bo_ref,
+    out_ref,
+    a_buf, w_tiled, proj_l, proj_r, l_send, l_all, r_all, lt_f32, lt, outer, lhs, outs,
+    load_sem, r_recv, up_sem, down_sem, side_sem, l_send_sem, l_recv, core_send,
+):
+    n_seq, n_res, depth, s_dev, block, chunks, width, channels, proj = dims
+    pack = LANES // proj
+    quads = block // pack
+    total = n_seq * s_dev
+    p = lax.axis_index("seq")
+    r = lax.axis_index("res")
+    rows = n_seq // depth
+    z = p // depth
+    y = p % depth
+    side = z * depth + (depth - 1 - y)
+
+    loads = []
+    for k in range(chunks):
+        load = pltpu.make_async_copy(
+            a_hbm.at[:, pl.ds(k * block, block), :], a_buf.at[k], load_sem.at[k]
+        )
+        load.start()
+        loads.append(load)
+
+    barrier = pltpu.get_barrier_semaphore()
+    for d in range(1, n_seq):
+        pl.semaphore_signal(
+            barrier, inc=1, device_id={"seq": lax.rem(p + d, n_seq)}, device_id_type=MESH
+        )
+    pl.semaphore_signal(barrier, inc=1, device_id={"res": 1 - r}, device_id_type=MESH)
+
+    def tile4(v):
+        return jnp.concatenate([v] * pack, axis=1)
+
+    w_tiled[:, :LANES] = tile4(wl_ref[...].astype(jnp.float32)).astype(jnp.bfloat16)
+    w_tiled[:, LANES:] = tile4(wr_ref[...].astype(jnp.float32)).astype(jnp.bfloat16)
+    bias_l = tile4(bl_ref[...])
+    bias_r = tile4(br_ref[...])
+    gain = gain_ref[...]
+    beta = beta_ref[...]
+    lane = lax.broadcasted_iota(jnp.int32, (s_dev, LANES), 1) // proj
+
+    def copy_r(k, slot, sem, target):
+        return pltpu.make_async_remote_copy(
+            src_ref=r_all.at[k, slot],
+            dst_ref=r_all.at[k, slot],
+            send_sem=sem.at[k, slot],
+            recv_sem=r_recv.at[k, slot],
+            device_id={"seq": target},
+            device_id_type=MESH,
+        )
+
+    def copy_up(k, slot):
+        return copy_r(k, slot, up_sem, p + depth)
+
+    def copy_down(k, slot):
+        return copy_r(k, slot, down_sem, p - depth)
+
+    def copy_side(k, slot):
+        return copy_r(k, slot, side_sem, side)
+
+    def copy_l(k):
+        return pltpu.make_async_remote_copy(
+            src_ref=l_send.at[k],
+            dst_ref=l_all.at[p],
+            send_sem=l_send_sem.at[k],
+            recv_sem=l_recv.at[p],
+            device_id={"seq": r * chunks + k},
+            device_id_type=MESH,
+        )
+
+    def copy_core(slot):
+        return pltpu.make_async_remote_copy(
+            src_ref=l_all.at[slot],
+            dst_ref=l_all.at[slot],
+            send_sem=core_send.at[slot],
+            recv_sem=l_recv.at[slot],
+            device_id={"res": 1 - r},
+            device_id_type=MESH,
+        )
+
+    seqs = 16
+    for k in range(chunks):
+        loads[k].wait()
+
+        def norm_step(t, carry, k=k):
+            values = a_buf[k, pl.ds(t * seqs, seqs)].reshape(seqs * block, channels)
+            values = values.astype(jnp.float32)
+            center = jnp.mean(values, axis=-1, keepdims=True)
+            values = values - center
+            spread = jnp.mean(jnp.square(values), axis=-1, keepdims=True)
+            normed = (values * lax.rsqrt(spread + 1e-05) * gain + beta).astype(jnp.bfloat16)
+            result = jnp.dot(normed, w_tiled[...], preferred_element_type=jnp.float32)
+            here = pl.ds(t * (seqs * block), seqs * block)
+            proj_l[here, :] = result[:, :LANES] + bias_l
+            proj_r[here, :] = result[:, LANES:] + bias_r
+            return carry
+
+        lax.fori_loop(0, s_dev // seqs, norm_step, 0)
+
+        for q in range(quads):
+            columns = slice(q * LANES, (q + 1) * LANES)
+
+            def merge(ref):
+                merged = ref[pl.ds(q * pack, s_dev, stride=block), :]
+                for m in range(1, pack):
+                    merged = jnp.where(
+                        lane == m, ref[pl.ds(q * pack + m, s_dev, stride=block), :], merged
+                    )
+                return merged.astype(jnp.bfloat16)
+
+            r_all[k, p, :, columns] = merge(proj_r)
+            l_send[k, :, columns] = merge(proj_l)
+
+        if k == 0:
+            pl.semaphore_wait(barrier, n_seq)
+
+        @pl.when(z + 1 < rows)
+        def _():
+            copy_up(k, p).start()
+
+        @pl.when(z > 0)
+        def _():
+            copy_down(k, p).start()
+
+        copy_side(k, p).start()
+
+        @pl.when(r * chunks + k != p)
+        def _():
+            copy_l(k).start()
+
+        @pl.when(r * chunks + k == p)
+        def _():
+            l_all[p] = l_send[k]
+
+    def forward(k):
+        for d in range(1, rows):
+            @pl.when(z - d >= 0)
+            def _():
+                slot = p - d * depth
+                copy_down(k, slot).wait_recv()
+                copy_side(k, slot).start()
+
+                @pl.when(z + 1 < rows)
+                def _():
+                    copy_up(k, slot).start()
+
+            @pl.when(z + d < rows)
+            def _():
+                slot = p + d * depth
+                copy_down(k, slot).wait_recv()
+                copy_side(k, slot).start()
+
+                @pl.when(z > 0)
+                def _():
+                    copy_down(k, slot).start()
+
+    def gather_left():
+        owner = p // chunks == r
+        for d in range(n_seq):
+            slot = lax.rem(p + d, n_seq)
+
+            @pl.when(owner)
+            def _():
+                if d > 0:
+                    copy_core(slot).wait_recv()
+                copy_core(slot).start()
+
+            @pl.when(jnp.logical_not(owner))
+            def _():
+                copy_core(slot).wait_recv()
+
+        left = l_all[...].reshape(total, block * proj)
+        for t in range(total // LANES):
+            lt_f32[t] = jnp.transpose(left[t * LANES : (t + 1) * LANES].astype(jnp.float32))
+            for c in range(proj):
+                lt[c * block : (c + 1) * block, t * LANES : (t + 1) * LANES] = lt_f32[
+                    t, pl.ds(c, block, stride=proj), :
+                ].astype(jnp.bfloat16)
+
+    high = (lax.broadcasted_iota(jnp.int32, (block, LANES), 1) // (2 * proj)) == 1
+    odd = ((lax.broadcasted_iota(jnp.int32, (block, LANES), 1) // proj) % 2) == 1
+
+    def compute(k):
+        for zz in range(rows):
+            copy_side(k, zz * depth + (depth - 1 - y)).wait_recv()
+        right = r_all[k].reshape(total, block * proj)
+        outer[...] = jnp.dot(lt[...], right, preferred_element_type=jnp.float32)
+
+        def regroup(cq, carry):
+            for jq in range(quads):
+                v = [
+                    outer[pl.ds((cq * pack + m) * block, block), jq * LANES : (jq + 1) * LANES]
+                    for m in range(pack)
+                ]
+                a0 = jnp.where(high, pltpu.roll(v[2], 2 * proj, 1), v[0])
+                a2 = jnp.where(high, v[2], pltpu.roll(v[0], 2 * proj, 1))
+                a1 = jnp.where(high, pltpu.roll(v[3], 2 * proj, 1), v[1])
+                a3 = jnp.where(high, v[3], pltpu.roll(v[1], 2 * proj, 1))
+                t = [
+                    jnp.where(odd, pltpu.roll(a1, proj, 1), a0),
+                    jnp.where(odd, a1, pltpu.roll(a0, 3 * proj, 1)),
+                    jnp.where(odd, pltpu.roll(a3, proj, 1), a2),
+                    jnp.where(odd, a3, pltpu.roll(a2, 3 * proj, 1)),
+                ]
+                for m in range(pack):
+                    lhs[
+                        (jq * pack + m) * block : (jq * pack + m + 1) * block,
+                        pl.ds(pl.multiple_of(cq * LANES, LANES), LANES),
+                    ] = t[m].astype(jnp.bfloat16)
+            return carry
+
+        lax.fori_loop(0, proj // pack, regroup, 0)
+        outs[...] = (
+            jnp.dot(lhs[...], w_ref[...], preferred_element_type=jnp.float32) * (1.0 / total)
+            + bo_ref[...]
+        )
+        for i in range(block):
+            out_ref[i, pl.ds(k * block, block), :] = outs[
+                pl.ds(i, block, stride=block), :
+            ].astype(jnp.bfloat16)
+
+    forward(0)
+    gather_left()
+    for k in range(chunks):
+        if k + 1 < chunks:
+            forward(k + 1)
+        compute(k)
+
+    owner = p // chunks == r
+    for k in range(chunks):
+        @pl.when(r * chunks + k != p)
+        def _():
+            copy_l(k).wait_send()
+
+        for zz in range(rows):
+            slot = zz * depth + y
+            copy_side(k, slot).wait_send()
+
+            @pl.when(jnp.logical_and(zz <= z, z + 1 < rows))
+            def _():
+                copy_up(k, slot).wait_send()
+
+            @pl.when(jnp.logical_and(zz >= z, z > 0))
+            def _():
+                copy_down(k, slot).wait_send()
+
+    @pl.when(owner)
+    def _():
+        for slot in range(n_seq):
+            copy_core(slot).wait_send()
+
+
+def shards(n_seq, n_res, alignment, ln_gain, ln_bias, w_left, bias_left, w_right, bias_right, w_out, bias_out):
+    s_dev, width, channels = alignment.shape
+    proj = w_left.shape[1]
+    out_width = w_out.shape[1]
+    block = width * n_res // n_seq
+    depth = 2
+    fits = (
+        n_res == 2
+        and n_seq % depth == 0
+        and block % 16 == 0
+        and width % block == 0
+        and proj * 4 == LANES
+        and out_width == LANES
+        and s_dev % 16 == 0
+        and (n_seq * s_dev) % LANES == 0
+    )
+    if not fits:
+        return plain(
+            alignment, ln_gain, ln_bias, w_left, bias_left, w_right, bias_right, w_out, bias_out
+        )
+    chunks = width // block
+    total = n_seq * s_dev
+    dims = (n_seq, n_res, depth, s_dev, block, chunks, width, channels, proj)
+    vmem = pl.BlockSpec(memory_space=pltpu.VMEM)
+    wide = block * proj
+    return pl.pallas_call(
+        functools.partial(fused_kernel, dims),
+        out_shape=jax.ShapeDtypeStruct((block, width, out_width), jnp.bfloat16),
+        in_specs=[pl.BlockSpec(memory_space=pl.ANY)] + [vmem] * 8,
+        out_specs=vmem,
+        scratch_shapes=[
+            pltpu.VMEM((chunks, s_dev, block, channels), jnp.bfloat16),
+            pltpu.VMEM((channels, 2 * LANES), jnp.bfloat16),
+            pltpu.VMEM((s_dev * block, LANES), jnp.float32),
+            pltpu.VMEM((s_dev * block, LANES), jnp.float32),
+            pltpu.VMEM((chunks, s_dev, wide), jnp.bfloat16),
+            pltpu.VMEM((n_seq, s_dev, wide), jnp.bfloat16),
+            pltpu.VMEM((chunks, n_seq, s_dev, wide), jnp.bfloat16),
+            pltpu.VMEM((total // LANES, wide, LANES), jnp.float32),
+            pltpu.VMEM((wide, total), jnp.bfloat16),
+            pltpu.VMEM((wide, wide), jnp.float32),
+            pltpu.VMEM((block * block, proj * proj), jnp.bfloat16),
+            pltpu.VMEM((block * block, out_width), jnp.float32),
+            pltpu.SemaphoreType.DMA((chunks,)),
+            pltpu.SemaphoreType.DMA((chunks, n_seq)),
+            pltpu.SemaphoreType.DMA((chunks, n_seq)),
+            pltpu.SemaphoreType.DMA((chunks, n_seq)),
+            pltpu.SemaphoreType.DMA((chunks, n_seq)),
+            pltpu.SemaphoreType.DMA((chunks,)),
+            pltpu.SemaphoreType.DMA((n_seq,)),
+            pltpu.SemaphoreType.DMA((n_seq,)),
+        ],
+        compiler_params=pltpu.CompilerParams(
+            collective_id=0, has_side_effects=True, vmem_limit_bytes=40 * 1024 * 1024
+        ),
+        name="outer_mean",
+    )(
+        alignment,
+        ln_gain.reshape(1, -1),
+        ln_bias.reshape(1, -1),
+        w_left,
+        bias_left.reshape(1, -1),
+        w_right,
+        bias_right.reshape(1, -1),
+        w_out,
+        bias_out.reshape(1, -1),
+    )
+
+
 def solution(mesh):
     return jax.shard_map(
-        shards,
+        functools.partial(shards, mesh.shape["seq"], mesh.shape["res"]),
         mesh=mesh,
         in_specs=(P(("group", "seq"), "res", None), P(), P(), P(), P(), P(), P(), P(), P()),
         out_specs=P(("group", "seq"), "res", None),

time: 161 us -> 54.1 us (0.34)
  waiting for transfers between devices: 90.7 us -> 0 us
  Pallas kernels: 0 us -> 45.5 us
  matrix products: 31.1 us -> 0 us
  between operations: 13.6 us -> 0.02 us
  other arithmetic: 8.18 us -> 0 us
  local copies, waits for them, and re-layouts: 14.7 us -> 8.24 us
  blocking collectives: 2.39 us -> 0 us
    reduce_scatter x1 -> x0, waiting for transfers between devices: 90.7 us -> none  [shards(): lax.psum_scatter(pair_tile(columns, right_rows, weight_cube, lax.axis_siz...]
    pallas_call x0 -> x1, Pallas kernels: none -> 45.5 us  [shards(): pl.pallas_call(functools.partial(fused_kernel, dims), out_shape=jax.Shape...]
    dot_general x18 -> x0, matrix products: 31.1 us -> none  [the longest x8 19.5 us: one_block(): jnp.einsum('icej,ceo->ijo', outers, weight_cube, preferred_element_type=j...]
    another operation x8 -> x0, local copies, waits for them, and re-layouts: 7.64 us -> none
    unnamed x20 -> x17, local copies, waits for them, and re-layouts: 1.33 us -> 8.24 us
    reduce_sum x2 -> x0, other arithmetic: 4.87 us -> none  [the longest x1 2.53 us: normalize(): spread = jnp.mean(jnp.square(values - center), axis=-1, keepdims=True)]
    convert_element_type x2 -> x0, other arithmetic: 3.29 us -> none  [the longest x1 1.82 us: shards(): return (summed / (sequences * devices_seq) + bias_out).astype(jnp.bfloat16)]
    all_gather x1 -> x0, blocking collectives: 2.39 us -> none  [shards(): columns = lax.all_gather(left_rows, 'res', axis=1, tiled=True)]
  transfers between devices with their start and end apart: 1 -> 0, of which waited for: 1 -> 0; matrix products, arithmetic and copies ran while one was open for 0% -> 0% of each run, Pallas kernels for 0% -> 0%
where the time goes in v1:
time: 54.1 us; the launch traced here: 53.7 us
  Pallas kernels  45.5 us (84%)
  local copies, waits for them, and re-layouts  8.24 us (15%)
    pallas_call x1, Pallas kernels, shards(): pl.pallas_call(functools.partial(fused_kernel, dims), out_shape=jax.Shape...  45.5 us
    unnamed x17, local copies, waits for them, and re-layouts  8.24 us

profile of v1, /device:TPU:0, one launch (start us, length us, event | category | flops | bytes accessed | tf_op | source)
XLA Modules:
  0.0 53.7 jit_solution(17736674181740125208)
XLA Ops:
  0.0 0.8 %copy.10.wl_ref = bf16[256,32]{1,0:T(8,128)(2,1)S(1)} copy(bf16[256,32]{0,1:T(8,128)(2,1)} %param.12) | data formatting | bytes 32768 | tf_op args[3]
  0.8 0.8 %copy.11.wr_ref = bf16[256,32]{1,0:T(8,128)(2,1)S(1)} copy(bf16[256,32]{0,1:T(8,128)(2,1)} %param.14) | data formatting | bytes 32768 | tf_op args[5]
  1.7 0.0 copy-start
  1.7 1.6 %copy-done = bf16[64,64,256]{2,1,0:T(8,128)(2,1)S(1)} copy-done((bf16[64,64,256]{2,1,0:T(8,128)(2,1)S(1)}, bf16[64,64,256]{2,1,0:T(8,128)(2,1)}, u32[]{:S(2)}) %copy-start) | copy-done | bytes 2097176
  3.3 0.0 copy-start.1
  3.3 0.9 %copy-done.1 = bf16[1024,128]{1,0:T(8,128)(2,1)S(1)} copy-done((bf16[1024,128]{1,0:T(8,128)(2,1)S(1)}, bf16[1024,128]{1,0:T(8,128)(2,1)}, u32[]{:S(2)}) %copy-start.1) | copy-done | bytes 262168
  4.2 0.0 copy-start.2
  4.2 0.7 %copy-done.2 = f32[256]{0:T(256)S(1)} copy-done((f32[256]{0:T(256)S(1)}, f32[256]{0:T(256)}, u32[]{:S(2)}) %copy-start.2) | copy-done | bytes 1048
  4.9 0.0 copy-start.3
  4.9 0.7 %copy-done.3 = f32[256]{0:T(256)S(1)} copy-done((f32[256]{0:T(256)S(1)}, f32[256]{0:T(256)}, u32[]{:S(2)}) %copy-start.3) | copy-done | bytes 1048
  5.6 0.0 copy-start.4
  5.6 0.7 %copy-done.4 = f32[32]{0:T(128)S(1)} copy-done((f32[32]{0:T(128)S(1)}, f32[32]{0:T(128)}, u32[]{:S(2)}) %copy-start.4) | copy-done | bytes 152
  6.2 0.0 copy-start.5
  6.2 0.7 %copy-done.5 = f32[32]{0:T(128)S(1)} copy-done((f32[32]{0:T(128)S(1)}, f32[32]{0:T(128)}, u32[]{:S(2)}) %copy-start.5) | copy-done | bytes 152
  6.9 0.0 copy-start.6
  6.9 0.7 %copy-done.6 = f32[128]{0:T(128)S(1)} copy-done((f32[128]{0:T(128)S(1)}, f32[128]{0:T(128)}, u32[]{:S(2)}) %copy-start.6) | copy-done | bytes 536
  7.5 45.5 %outer_mean.1 = bf16[16,64,128]{2,1,0:T(8,128)(2,1)S(1)} custom-call(bf16[64,64,256]{2,1,0:T(8,128)(2,1)S(1)} %copy-done, f32[1,256]{1,0:T(1,128)S(1)} %bitcast.5, f32[1,256]{1,0:T(1,128)S(1)} %bitcast.6, bf16[256,32]{1,0:T(8,128)(2,1)S(1)} %copy.10.wl_ref, f32[1,32]{1,0:T(1,128)S(1)} %bitcast.7, bf16[256,32]{1,0:T(8,128)(2,1)S(1)} %copy.11.wr_ref, ...), custom_call_target="tpu_custom_call" | custom-call | tf_op jit(solution)/shard_map/outer_mean/pallas_call | solution.py:350
  53.0 0.7 %copy.13 = bf16[16,64,128]{2,1,0:T(8,128)(2,1)} copy(bf16[16,64,128]{2,1,0:T(8,128)(2,1)S(1)} %outer_mean.1) | data formatting | bytes 524288
Async XLA Ops:
  1.7 1.6 %copy-start = (bf16[64,64,256]{2,1,0:T(8,128)(2,1)S(1)}, bf16[64,64,256]{2,1,0:T(8,128)(2,1)}, u32[]{:S(2)}) copy-start(bf16[64,64,256]{2,1,0:T(8,128)(2,1)} %a_hbm.1) | copy-start | bytes 6291460
  3.3 0.9 %copy-start.1 = (bf16[1024,128]{1,0:T(8,128)(2,1)S(1)}, bf16[1024,128]{1,0:T(8,128)(2,1)}, u32[]{:S(2)}) copy-start(bf16[1024,128]{1,0:T(8,128)(2,1)} %w_ref.1) | copy-start | bytes 786436
  4.2 0.7 %copy-start.2 = (f32[256]{0:T(256)S(1)}, f32[256]{0:T(256)}, u32[]{:S(2)}) copy-start(f32[256]{0:T(256)} %param.10) | copy-start | bytes 3076
  4.9 0.7 %copy-start.3 = (f32[256]{0:T(256)S(1)}, f32[256]{0:T(256)}, u32[]{:S(2)}) copy-start(f32[256]{0:T(256)} %param.11) | copy-start | bytes 3076
  5.6 0.7 %copy-start.4 = (f32[32]{0:T(128)S(1)}, f32[32]{0:T(128)}, u32[]{:S(2)}) copy-start(f32[32]{0:T(128)} %param.13) | copy-start | bytes 388
  6.2 0.7 %copy-start.5 = (f32[32]{0:T(128)S(1)}, f32[32]{0:T(128)}, u32[]{:S(2)}) copy-start(f32[32]{0:T(128)} %param.15) | copy-start | bytes 388
  6.9 0.7 %copy-start.6 = (f32[128]{0:T(128)S(1)}, f32[128]{0:T(128)}, u32[]{:S(2)}) copy-start(f32[128]{0:T(128)} %param.17) | copy-start | bytes 1540

commit v2 on v1

--- a/solution.py
+++ b/solution.py
@@ -69,10 +69,11 @@
 
 def fused_kernel(
     dims,
-    a_hbm, gain_ref, beta_ref, wl_ref, bl_ref, wr_ref, br_ref, w_ref, bo_ref,
+    a_hbm, gain_hbm, beta_hbm, wl_hbm, bl_hbm, wr_hbm, br_hbm, w_hbm, bo_hbm,
     out_ref,
+    gain_ref, beta_ref, wl_ref, bl_ref, wr_ref, br_ref, w_ref, bo_ref,
     a_buf, w_tiled, proj_l, proj_r, l_send, l_all, r_all, lt_f32, lt, outer, lhs, outs,
-    load_sem, r_recv, up_sem, down_sem, side_sem, l_send_sem, l_recv, core_send,
+    load_sem, small_sem, r_recv, up_sem, down_sem, side_sem, l_send_sem, l_recv, core_send,
 ):
     n_seq, n_res, depth, s_dev, block, chunks, width, channels, proj = dims
     pack = LANES // proj
@@ -85,6 +86,22 @@
     y = p % depth
     side = z * depth + (depth - 1 - y)
 
+    small = []
+    for n, (hbm, ref) in enumerate(
+        [
+            (gain_hbm, gain_ref),
+            (beta_hbm, beta_ref),
+            (wl_hbm, wl_ref),
+            (bl_hbm, bl_ref),
+            (wr_hbm, wr_ref),
+            (br_hbm, br_ref),
+            (w_hbm, w_ref),
+            (bo_hbm, bo_ref),
+        ]
+    ):
+        small.append(pltpu.make_async_copy(hbm, ref, small_sem.at[n]))
+    for load in small[:6]:
+        load.start()
     loads = []
     for k in range(chunks):
         load = pltpu.make_async_copy(
@@ -92,6 +109,8 @@
         )
         load.start()
         loads.append(load)
+    for load in small[6:]:
+        load.start()
 
     barrier = pltpu.get_barrier_semaphore()
     for d in range(1, n_seq):
@@ -103,8 +122,10 @@
     def tile4(v):
         return jnp.concatenate([v] * pack, axis=1)
 
-    w_tiled[:, :LANES] = tile4(wl_ref[...].astype(jnp.float32)).astype(jnp.bfloat16)
-    w_tiled[:, LANES:] = tile4(wr_ref[...].astype(jnp.float32)).astype(jnp.bfloat16)
+    for load in small[:6]:
+        load.wait()
+    both = [wl_ref[...].astype(jnp.float32)] * pack + [wr_ref[...].astype(jnp.float32)] * pack
+    w_tiled[...] = jnp.transpose(jnp.concatenate(both, axis=0)).astype(jnp.bfloat16)
     bias_l = tile4(bl_ref[...])
     bias_r = tile4(br_ref[...])
     gain = gain_ref[...]
@@ -149,6 +170,34 @@
             device_id={"res": 1 - r},
             device_id_type=MESH,
         )
+
+    def hop(k, d):
+        @pl.when(z - d >= 0)
+        def _():
+            slot = p - d * depth
+            copy_down(k, slot).wait_recv()
+
+            @pl.when(z + 1 < rows)
+            def _():
+                copy_up(k, slot).start()
+
+            copy_side(k, slot).start()
+
+        @pl.when(z + d < rows)
+        def _():
+            slot = p + d * depth
+            copy_down(k, slot).wait_recv()
+
+            @pl.when(z > 0)
+            def _():
+                copy_down(k, slot).start()
+
+            copy_side(k, slot).start()
+
+    def wave(t):
+        for d in range(1, rows):
+            if 0 <= t - d < chunks:
+                hop(t - d, d)
 
     seqs = 16
     for k in range(chunks):
@@ -204,27 +253,7 @@
         def _():
             l_all[p] = l_send[k]
 
-    def forward(k):
-        for d in range(1, rows):
-            @pl.when(z - d >= 0)
-            def _():
-                slot = p - d * depth
-                copy_down(k, slot).wait_recv()
-                copy_side(k, slot).start()
-
-                @pl.when(z + 1 < rows)
-                def _():
-                    copy_up(k, slot).start()
-
-            @pl.when(z + d < rows)
-            def _():
-                slot = p + d * depth
-                copy_down(k, slot).wait_recv()
-                copy_side(k, slot).start()
-
-                @pl.when(z > 0)
-                def _():
-                    copy_down(k, slot).start()
+        wave(k)
 
     def gather_left():
         owner = p // chunks == r
@@ -291,11 +320,15 @@
                 pl.ds(i, block, stride=block), :
             ].astype(jnp.bfloat16)
 
-    forward(0)
+    wave(chunks)
     gather_left()
+    done = chunks + 1
+    for load in small[6:]:
+        load.wait()
     for k in range(chunks):
-        if k + 1 < chunks:
-            forward(k + 1)
+        while done < chunks + rows - 1 and done - (rows - 1) <= k + 1:
+            wave(done)
+            done += 1
         compute(k)
 
     owner = p // chunks == r
@@ -350,9 +383,17 @@
     return pl.pallas_call(
         functools.partial(fused_kernel, dims),
         out_shape=jax.ShapeDtypeStruct((block, width, out_width), jnp.bfloat16),
-        in_specs=[pl.BlockSpec(memory_space=pl.ANY)] + [vmem] * 8,
+        in_specs=[pl.BlockSpec(memory_space=pl.ANY)] * 9,
         out_specs=vmem,
         scratch_shapes=[
+            pltpu.VMEM((1, channels), jnp.float32),
+            pltpu.VMEM((1, channels), jnp.float32),
+            pltpu.VMEM((proj, channels), jnp.bfloat16),
+            pltpu.VMEM((1, proj), jnp.float32),
+            pltpu.VMEM((proj, channels), jnp.bfloat16),
+            pltpu.VMEM((1, proj), jnp.float32),
+            pltpu.VMEM((proj * proj, out_width), jnp.bfloat16),
+            pltpu.VMEM((1, out_width), jnp.float32),
             pltpu.VMEM((chunks, s_dev, block, channels), jnp.bfloat16),
             pltpu.VMEM((channels, 2 * LANES), jnp.bfloat16),
             pltpu.VMEM((s_dev * block, LANES), jnp.float32),
@@ -366,6 +407,7 @@
             pltpu.VMEM((block * block, proj * proj), jnp.bfloat16),
             pltpu.VMEM((block * block, out_width), jnp.float32),
             pltpu.SemaphoreType.DMA((chunks,)),
+            pltpu.SemaphoreType.DMA((8,)),
             pltpu.SemaphoreType.DMA((chunks, n_seq)),
             pltpu.SemaphoreType.DMA((chunks, n_seq)),
             pltpu.SemaphoreType.DMA((chunks, n_seq)),
@@ -375,16 +417,16 @@
             pltpu.SemaphoreType.DMA((n_seq,)),
         ],
         compiler_params=pltpu.CompilerParams(
-            collective_id=0, has_side_effects=True, vmem_limit_bytes=40 * 1024 * 1024
+            collective_id=0, has_side_effects=True, vmem_limit_bytes=60 * 1024 * 1024
         ),
         name="outer_mean",
     )(
         alignment,
         ln_gain.reshape(1, -1),
         ln_bias.reshape(1, -1),
-        w_left,
+        w_left.T,
         bias_left.reshape(1, -1),
-        w_right,
+        w_right.T,
         bias_right.reshape(1, -1),
         w_out,
         bias_out.reshape(1, -1),

time: 54.1 us -> 42.2 us (0.78)
  local copies, waits for them, and re-layouts: 8.24 us -> 1.67 us
  Pallas kernels: 45.5 us -> 40.4 us
    unnamed x17 -> x1, local copies, waits for them, and re-layouts: 8.24 us -> 1.67 us
    pallas_call x1, Pallas kernels: 45.5 us -> 40.4 us  [shards(): pl.pallas_call(functools.partial(fused_kernel, dims), out_shape=jax.Shape...]
where the time goes in v2:
time: 42.2 us; the launch traced here: 42.1 us
  Pallas kernels  40.4 us (96%)
  local copies, waits for them, and re-layouts  1.67 us (4%)
    pallas_call x1, Pallas kernels, shards(): pl.pallas_call(functools.partial(fused_kernel, dims), out_shape=jax.Shape...  40.4 us
    unnamed x1, local copies, waits for them, and re-layouts  1.67 us

profile of v2, /device:TPU:0, one launch (start us, length us, event | category | flops | bytes accessed | tf_op | source)
XLA Modules:
  0.0 42.1 jit_solution(13921995940794042908)
XLA Ops:
  0.0 40.4 %outer_mean.1 = bf16[16,64,128]{2,1,0:T(8,128)(2,1)} custom-call(bf16[64,64,256]{2,1,0:T(8,128)(2,1)} %a_hbm.1, f32[1,256]{1,0:T(1,128)} %bitcast.9, f32[1,256]{1,0:T(1,128)} %bitcast.10, bf16[32,256]{1,0:T(8,128)(2,1)} %bitcast.7, f32[1,32]{1,0:T(1,128)} %bitcast.11, bf16[32,256]{1,0:T(8,128)(2,1)} %bitcast.8, f32[1,32]{1,0:T(1,128)} %bitcast.12, ...), custom_call_target="tpu_custom_call" | custom-call | tf_op jit(solution)/shard_map/outer_mean/pallas_call | solution.py:383
  40.4 1.7 %copy.11 = bf16[16,64,128]{2,1,0:T(8,128)(2,1)} copy(bf16[16,64,128]{2,1,0:T(8,128)(2,1)} %outer_mean.1) | data formatting | bytes 524288

commit v3 on v2

--- a/solution.py
+++ b/solution.py
@@ -216,7 +216,7 @@
             proj_r[here, :] = result[:, LANES:] + bias_r
             return carry
 
-        lax.fori_loop(0, s_dev // seqs, norm_step, 0)
+        lax.fori_loop(0, s_dev // seqs, norm_step, 0, unroll=True)
 
         for q in range(quads):
             columns = slice(q * LANES, (q + 1) * LANES)
@@ -235,6 +235,8 @@
         if k == 0:
             pl.semaphore_wait(barrier, n_seq)
 
+        copy_side(k, p).start()
+
         @pl.when(z + 1 < rows)
         def _():
             copy_up(k, p).start()
@@ -242,8 +244,6 @@
         @pl.when(z > 0)
         def _():
             copy_down(k, p).start()
-
-        copy_side(k, p).start()
 
         @pl.when(r * chunks + k != p)
         def _():
@@ -310,7 +310,7 @@
                     ] = t[m].astype(jnp.bfloat16)
             return carry
 
-        lax.fori_loop(0, proj // pack, regroup, 0)
+        lax.fori_loop(0, proj // pack, regroup, 0, unroll=True)
         outs[...] = (
             jnp.dot(lhs[...], w_ref[...], preferred_element_type=jnp.float32) * (1.0 / total)
             + bo_ref[...]
@@ -326,7 +326,7 @@
     for load in small[6:]:
         load.wait()
     for k in range(chunks):
-        while done < chunks + rows - 1 and done - (rows - 1) <= k + 1:
+        while done < chunks + rows - 1 and done - (rows - 1) <= k + 2:
             wave(done)
             done += 1
         compute(k)

time: 42.2 us -> 38.7 us (0.917)
  Pallas kernels: 40.4 us -> 36.9 us
    pallas_call x1, Pallas kernels: 40.4 us -> 36.9 us  [shards(): pl.pallas_call(functools.partial(fused_kernel, dims), out_shape=jax.Shape...]
where the time goes in v3:
time: 38.7 us; the launch traced here: 38.6 us
  Pallas kernels  36.9 us (95%)
  local copies, waits for them, and re-layouts  1.67 us (4%)
    pallas_call x1, Pallas kernels, shards(): pl.pallas_call(functools.partial(fused_kernel, dims), out_shape=jax.Shape...  36.9 us
    unnamed x1, local copies, waits for them, and re-layouts  1.67 us

profile of v3, /device:TPU:0, one launch (start us, length us, event | category | flops | bytes accessed | tf_op | source)
XLA Modules:
  0.0 38.6 jit_solution(9214000387095872136)
XLA Ops:
  0.0 36.9 %outer_mean.1 = bf16[16,64,128]{2,1,0:T(8,128)(2,1)} custom-call(bf16[64,64,256]{2,1,0:T(8,128)(2,1)} %a_hbm.1, f32[1,256]{1,0:T(1,128)} %bitcast.9, f32[1,256]{1,0:T(1,128)} %bitcast.10, bf16[32,256]{1,0:T(8,128)(2,1)} %bitcast.7, f32[1,32]{1,0:T(1,128)} %bitcast.11, bf16[32,256]{1,0:T(8,128)(2,1)} %bitcast.8, f32[1,32]{1,0:T(1,128)} %bitcast.12, ...), custom_call_target="tpu_custom_call" | custom-call | tf_op jit(solution)/shard_map/outer_mean/pallas_call | solution.py:383
  36.9 1.7 %copy.11 = bf16[16,64,128]{2,1,0:T(8,128)(2,1)} copy(bf16[16,64,128]{2,1,0:T(8,128)(2,1)} %outer_mean.1) | data formatting | bytes 524288
